TPU v7x, 512 devices: a whole 4x8x8 slice. The times are simulated.
512 devices in a mesh: ens: 4 (over y_hi), lat: 8 (over y_lo, x), lon: 16 (over z, core).
Axes of the slice: x: 4, y: 8 (y_hi: 4, y_lo: 2; y = y_hi * 2 + y_lo), z: 8, core: 2. Of those that a mesh axis runs over, the one named last changes fastest.
Arguments:
- initial_state: float32 [24, 128, 2048], P('ens', 'lat', 'lon'), parts along dimension 0, may hold values from -6 to 6
- diffusion: float32 [128, 2048], P('lat', 'lon'), may hold values from 0.05 to 0.2
- mixing: float32 [6, 6], replicated, may hold values from -0.3 to 0.3
- land_mask: int32 [128, 2048], P('lat', 'lon'), may hold values 0 or 1
- first_layer: bfloat16 [128, 54], replicated, may hold values from -0.875 to 0.875
- second_layer: bfloat16 [128, 128], replicated, may hold values from -0.5 to 0.5
- output_layer: bfloat16 [6, 128], replicated, may hold values from -0.5 to 0.5
- cotangent: float32 [24, 128, 2048], P('ens', 'lat', 'lon'), parts along dimension 0, may hold values from -20 to 20
- update_noise: float32 [96256], P('ens'), parts along dimension 0, may hold values from -0.15 to 0.15
Outputs:
- final_state: float32 [24, 128, 2048], P('ens', 'lat', 'lon'), parts along dimension 0
- initial_adjoint: float32 [24, 128, 2048], P('ens', 'lat', 'lon'), parts along dimension 0
- new_params: float32 [96256], P('ens'), parts along dimension 0
- noise_ratio: float32 [4], P('ens'), parts along dimension 0
There are 4 independent parts, one for each index of `ens`. A program takes and returns all parts, laid end to end along the dimension named above; an argument that names none is the same for every part. Nothing has to cross between parts.
All inputs are finite; a program needn't handle non-finite values. No bound on the sum of `land_mask` on one device may be relied on, other than what follows from the above.
Results may differ from a plain program's by a relative error of at most 0.0033.
Values sent between devices are 32-bit elements; how exact they have to be, the bound alone decides.
A program may use at most 64 MiB of HBM per device.

v0:
```python
import jax
import jax.numpy as jnp
from jax import lax
from jax.sharding import PartitionSpec as P

STEPS = 2
closure_dt = 0.1
learn_rate = 0.1
epsilon = 1e-06
offsets = [(row_shift, col_shift) for row_shift in (-1, 0, 1) for col_shift in (-1, 0, 1)]


def with_halo(value, sides, width, wrap):
    for axis, dim in sides:
        devices, length = (lax.axis_size(axis), value.shape[dim])
        up = [(i, (i + 1) % devices) for i in range(devices if wrap else devices - 1)]
        down = [(j, i) for i, j in up]
        last = lax.slice_in_dim(value, length - width, length, axis=dim)
        first = lax.slice_in_dim(value, 0, width, axis=dim)
        before = lax.ppermute(last, axis, up)
        after = lax.ppermute(first, axis, down)
        value = jnp.concatenate([before, value, after], axis=dim)
    return value


def contract_last(left, right):
    return lax.dot_general(
        left, right, (((1,), (1,)), ((), ())), preferred_element_type=jnp.float32
    )


def contract_first(left, right):
    return lax.dot_general(
        left, right, (((0,), (0,)), ((), ())), preferred_element_type=jnp.float32
    )


def build_patch(slab, rows, cols):
    return jnp.concatenate(
        [
            slab[:, 1 + row_shift : 1 + row_shift + rows, 1 + col_shift : 1 + col_shift + cols]
            for row_shift, col_shift in offsets
        ],
        axis=0,
    )


def hidden_layers(flat, first_layer, second_layer):
    hidden_one = jnp.tanh(jnp.dot(first_layer, flat, preferred_element_type=jnp.float32)).astype(
        jnp.bfloat16
    )
    hidden_two = jnp.tanh(
        jnp.dot(second_layer, hidden_one, preferred_element_type=jnp.float32)
    ).astype(jnp.bfloat16)
    return (hidden_one, hidden_two)


def forward_block(slab, mask_rows, diff_rows, mixing, first_layer, second_layer, output_layer):
    fields = slab.shape[0]
    rows = slab.shape[1] - 2
    cols = slab.shape[2] - 2
    count = rows * cols
    patch = build_patch(slab, rows, cols)
    centre = patch[4 * fields : 5 * fields]
    laplace = (
        patch[fields : 2 * fields]
        + patch[3 * fields : 4 * fields]
        + patch[5 * fields : 6 * fields]
        + patch[7 * fields : 8 * fields]
        - 4.0 * centre
    )
    flat = patch.reshape(9 * fields, count).astype(jnp.bfloat16)
    hidden_one, hidden_two = hidden_layers(flat, first_layer, second_layer)
    tendency = jnp.dot(output_layer, hidden_two, preferred_element_type=jnp.float32)
    mixed = jnp.dot(mixing, centre.reshape(fields, count), precision=lax.Precision.HIGHEST)
    update = (
        centre
        + diff_rows[None] * laplace
        + (mixed + closure_dt * tendency).reshape(fields, rows, cols)
    )
    return mask_rows[None] * update


def backward_block(
    slab, adjoint_rows, mask_rows, diff_rows, mixing, first_layer, second_layer, output_layer
):
    fields = slab.shape[0]
    rows = slab.shape[1] - 2
    cols = slab.shape[2] - 2
    count = rows * cols
    patch = build_patch(slab, rows, cols)
    flat = patch.reshape(9 * fields, count).astype(jnp.bfloat16)
    hidden_one, hidden_two = hidden_layers(flat, first_layer, second_layer)
    masked = (mask_rows[None] * adjoint_rows).reshape(fields, count)
    out_grad = (closure_dt * masked).astype(jnp.bfloat16)
    back_two = (
        contract_first(output_layer, out_grad) * (1.0 - jnp.square(hidden_two.astype(jnp.float32)))
    ).astype(jnp.bfloat16)
    back_one = (
        contract_first(second_layer, back_two) * (1.0 - jnp.square(hidden_one.astype(jnp.float32)))
    ).astype(jnp.bfloat16)
    patch_grad = contract_first(first_layer, back_one)
    direct = masked + lax.dot_general(
        mixing,
        masked,
        (((0,), (0,)), ((), ())),
        precision=lax.Precision.HIGHEST,
        preferred_element_type=jnp.float32,
    )
    spread = diff_rows.reshape(1, count) * masked
    blank = jnp.zeros_like(masked)
    extra = jnp.concatenate(
        [blank, spread, blank, spread, direct - 4.0 * spread, spread, blank, spread, blank], axis=0
    )
    patch_grad = (patch_grad + extra).reshape(9 * fields, rows, cols)
    grads = jnp.concatenate(
        [
            contract_last(back_one, flat).ravel(),
            contract_last(back_two, hidden_one).ravel(),
            contract_last(out_grad, hidden_two).ravel(),
        ]
    )
    return (patch_grad, grads)


def on_device(
    initial_state,
    diffusion,
    mixing,
    land_mask,
    first_layer,
    second_layer,
    output_layer,
    cotangent,
    update_noise,
):
    fields, rows, cols = initial_state.shape
    mask = land_mask.astype(jnp.float32)
    state = initial_state
    saved = []
    for step in range(STEPS):
        wide = with_halo(state, (("lon", 2),), 1, True)
        padded = with_halo(wide, (("lat", 1),), 1, False)
        saved.append(padded)
        state = forward_block(
            padded, mask, diffusion, mixing, first_layer, second_layer, output_layer
        )
    adjoint = cotangent
    local_grad = jnp.zeros((first_layer.size + second_layer.size + output_layer.size,), jnp.float32)
    for step in reversed(range(STEPS)):
        patch_grad, grads = backward_block(
            saved[step], adjoint, mask, diffusion, mixing, first_layer, second_layer, output_layer
        )
        local_grad = local_grad + grads
        wide_grad = with_halo(patch_grad, (("lon", 2),), 1, True)
        grad_pad = with_halo(wide_grad, (("lat", 1),), 1, False)
        total = jnp.zeros((fields, rows, cols), jnp.float32)
        for number, (row_shift, col_shift) in enumerate(offsets):
            total = (
                total
                + grad_pad[
                    number * fields : (number + 1) * fields,
                    1 - row_shift : 1 - row_shift + rows,
                    1 - col_shift : 1 - col_shift + cols,
                ]
            )
        adjoint = total
    params_count = local_grad.shape[0]
    band = lax.psum(local_grad, "lon")
    total_grad, band_square = lax.psum((band, jnp.sum(band * band)), "lat")
    grad_square = jnp.sum(total_grad * total_grad)
    noise_ratio = (band_square / (grad_square + epsilon)).reshape(1)
    params = jnp.concatenate(
        [
            first_layer.astype(jnp.float32).ravel(),
            second_layer.astype(jnp.float32).ravel(),
            output_layer.astype(jnp.float32).ravel(),
        ]
    )
    new_params = (
        params
        - learn_rate * total_grad / jnp.sqrt(grad_square / params_count + epsilon)
        + update_noise
    )
    return (state, adjoint, new_params, noise_ratio)


def solution(mesh):
    placed = (
        P("ens", "lat", "lon"),
        P("lat", "lon"),
        P(),
        P("lat", "lon"),
        P(),
        P(),
        P(),
        P("ens", "lat", "lon"),
        P("ens"),
    )
    return jax.shard_map(
        on_device,
        mesh=mesh,
        in_specs=placed,
        out_specs=(P("ens", "lat", "lon"), P("ens", "lat", "lon"), P("ens"), P("ens")),
        check_vma=False,
    )
```

profile of v0, /device:TPU:40, one launch (start us, length us, event | category | flops | bytes accessed | tf_op | source)
XLA Modules:
  0.0 304.6 jit_solution(4147958158141349705)
XLA Ops:
  8.2 8.5 %collective-permute-start.1 = (f32[6,16,1]{2,1,0:T(8,128)S(1)}, f32[6,16,1]{2,1,0:T(8,128)S(1)}, u32[]{:S(2)}, u32[]{:S(2)}) collective-permute-start(f32[6,16,1]{2,1,0:T(8,128)S(1)} %get-tuple-element.31), channel_id=1, source_target_pairs={{1,0},{2,1},{3,2},{4,3},{5,4},{6,5},{7,6},{8,7},{9,8},{10,9},{11,1... | collective-permute-start | bytes 1160 | tf_op jit(solution)/shard_map/ppermute | solution.py:21
  16.7 1.8 collective-permute-done
  18.6 5.5 %collective-permute-start.3 = (f32[6,1,130]{2,1,0:T(1,128)S(1)}, f32[6,1,130]{2,1,0:T(1,128)S(1)}, u32[]{:S(2)}, u32[]{:S(2)}) collective-permute-start(f32[6,1,130]{2,1,0:T(1,128)S(1)} %get-tuple-element.26), channel_id=1, source_target_pairs={{16,0},{32,16},{48,32},{64,48},{80,64},{96,80},{112,96},{17,1},{33... | collective-permute-start | bytes 9368 | tf_op jit(solution)/shard_map/ppermute | solution.py:21
  24.0 1.9 collective-permute-start.2
  26.7 5.0 %collective-permute-done.2 = f32[6,1,130]{2,1,0:T(1,128)S(1)} collective-permute-done((f32[6,1,130]{2,1,0:T(1,128)S(1)}, f32[6,1,130]{2,1,0:T(1,128)S(1)}, u32[]{:S(2)}, u32[]{:S(2)}) %collective-permute-start.2) | collective-permute-done | bytes 3152 | tf_op jit(solution)/shard_map/ppermute | solution.py:20
  35.5 3.0 collective-permute-start.5
  40.4 1.9 collective-permute-start.7
  42.3 3.9 %collective-permute-start.6 = (f32[6,1,130]{2,1,0:T(1,128)S(1)}, f32[6,1,130]{2,1,0:T(1,128)S(1)}, u32[]{:S(2)}, u32[]{:S(2)}) collective-permute-start(f32[6,1,130]{2,1,0:T(1,128)S(1)} %get-tuple-element.23), channel_id=1, source_target_pairs={{0,16},{16,32},{32,48},{48,64},{64,80},{80,96},{96,112},{1,17},{17... | collective-permute-start | bytes 9368 | tf_op jit(solution)/shard_map/ppermute | solution.py:20
  46.5 3.5 %collective-permute-done.6 = f32[6,1,130]{2,1,0:T(1,128)S(1)} collective-permute-done((f32[6,1,130]{2,1,0:T(1,128)S(1)}, f32[6,1,130]{2,1,0:T(1,128)S(1)}, u32[]{:S(2)}, u32[]{:S(2)}) %collective-permute-start.6) | collective-permute-done | bytes 3152 | tf_op jit(solution)/shard_map/ppermute | solution.py:20
  56.4 11.9 %concatenate.120 = f32[54,2048]{1,0:T(8,128)} concatenate(f32[6,2048]{1,0:T(8,128)S(1)} %broadcast.26, f32[6,2048]{1,0:T(8,128)S(1)} %bitcast_multiply_fusion.2, f32[6,2048]{1,0:T(8,128)S(1)} %broadcast.26, f32[6,2048]{1,0:T(8,128)S(1)} %bitcast_multiply_fusion.2, f32[6,2048]{1,0:T(8,128)} %fusion.13, f32[6,2048]{1,0:T(8,128)S(1)} %bitcast_multiply_fusion.2, ...), dimensions={0} | concatenate | bytes 884736 | tf_op jit(solution)/shard_map/concatenate | solution.py:112
  70.0 2.9 collective-permute-start.9
  74.0 5.0 %collective-permute-done.8 = f32[54,16,1]{2,1,0:T(8,128)S(1)} collective-permute-done((f32[54,16,1]{2,1,0:T(8,128)S(1)}, f32[54,16,1]{2,1,0:T(8,128)S(1)}, u32[]{:S(2)}, u32[]{:S(2)}) %collective-permute-start.8) | collective-permute-done | bytes 3488 | tf_op jit(solution)/shard_map/ppermute | solution.py:20
  80.0 2.0 collective-permute-start.10
  82.1 4.1 %collective-permute-start.11 = (f32[54,1,130]{2,1,0:T(1,128)}, f32[54,1,130]{2,1,0:T(1,128)}, u32[]{:S(2)}, u32[]{:S(2)}) collective-permute-start(f32[54,1,130]{2,1,0:T(1,128)} %get-tuple-element.15), channel_id=1, source_target_pairs={{0,16},{16,32},{32,48},{48,64},{64,80},{80,96},{96,112},{1,17},{17... | collective-permute-start | bytes 84248 | tf_op jit(solution)/shard_map/ppermute | solution.py:20
  86.5 4.2 %collective-permute-done.11 = f32[54,1,130]{2,1,0:T(1,128)} collective-permute-done((f32[54,1,130]{2,1,0:T(1,128)}, f32[54,1,130]{2,1,0:T(1,128)}, u32[]{:S(2)}, u32[]{:S(2)}) %collective-permute-start.11) | collective-permute-done | bytes 28112 | tf_op jit(solution)/shard_map/ppermute | solution.py:20
  95.1 2.9 collective-permute-start.13
  98.8 5.3 %collective-permute-done.12 = f32[54,16,1]{2,1,0:T(8,128)S(1)} collective-permute-done((f32[54,16,1]{2,1,0:T(8,128)S(1)}, f32[54,16,1]{2,1,0:T(8,128)S(1)}, u32[]{:S(2)}, u32[]{:S(2)}) %collective-permute-start.12) | collective-permute-done | bytes 3488 | tf_op jit(solution)/shard_map/ppermute | solution.py:20
  104.5 1.9 collective-permute-start.14
  106.4 3.9 %collective-permute-start.15 = (f32[54,1,130]{2,1,0:T(1,128)S(1)}, f32[54,1,130]{2,1,0:T(1,128)S(1)}, u32[]{:S(2)}, u32[]{:S(2)}) collective-permute-start(f32[54,1,130]{2,1,0:T(1,128)S(1)} %get-tuple-element.13), channel_id=1, source_target_pairs={{0,16},{16,32},{32,48},{48,64},{64,80},{80,96},{96,112},{1,17},{17... | collective-permute-start | bytes 84248 | tf_op jit(solution)/shard_map/ppermute | solution.py:20
  110.3 93.3 %all-reduce.3.cloned.1.call-done = f32[24064]{0:T(1024)} async-done(((f32[24064]{0:T(1024)}), f32[24064]{0:T(1024)}) %all-reduce.3.cloned.1.call-update) | async-done | bytes 96272 | tf_op jit(solution)/shard_map/psum | solution.py:169
  206.8 20.1 %psum.23 = f32[]{:T(128)} all-reduce(f32[]{:T(128)} %multiply_reduce_fusion), channel_id=1, replica_groups=mesh['ens'=4,'lat'=8,'lon'=16] {'lat'}, use_global_device_ids=true, to_apply=%region_4.0 | all-reduce | flops 1 | bytes 8 | tf_op jit(solution)/shard_map/psum | solution.py:170
  226.9 64.6 %all-reduce.5.cloned.1.call-done = f32[24064]{0:T(1024)} async-done(((f32[24064]{0:T(1024)}), f32[24064]{0:T(1024)}) %all-reduce.5.cloned.1.call-update) | async-done | bytes 96272 | tf_op jit(solution)/shard_map/psum | solution.py:170
  291.5 1.5 multiply_reduce_fusion.1
  295.1 1.6 subtract_add_fusion
  (135 shorter events, 26.8 us)
Async XLA Ops:
  7.2 18.8 %copy-start = (f32[6,6]{1,0:T(8,128)S(1)}, f32[6,6]{1,0:T(8,128)}, u32[]{:S(2)}) copy-start(f32[6,6]{1,0:T(8,128)} %param.11) | copy-start | bytes 436
  7.2 11.3 %copy-start.1 = (f32[6,16,128]{2,1,0:T(8,128)S(1)}, f32[6,16,128]{2,1,0:T(8,128)}, u32[]{:S(2)}) copy-start(f32[6,16,128]{2,1,0:T(8,128)} %param.9) | copy-start | bytes 147460
  7.2 196.4 %all-reduce.3.cloned.1.call-start = ((), (), s32[]{:S(2)}) async-start(), calls=%async_computation | async-start | bytes 196608 | tf_op jit(solution)/shard_map/psum | solution.py:169
  8.2 10.3 %collective-permute-start = (f32[6,16,1]{2,1,0:T(8,128)S(1)}, f32[6,16,1]{2,1,0:T(8,128)S(1)}, u32[]{:S(2)}, u32[]{:S(2)}) collective-permute-start(f32[6,16,1]{2,1,0:T(8,128)S(1)} %get-tuple-element.30), channel_id=1, source_target_pairs={{0,1},{1,2},{2,3},{3,4},{4,5},{5,6},{6,7},{7,8},{8,9},{9,10},{10,1... | collective-permute-start | bytes 1160 | tf_op jit(solution)/shard_map/ppermute | solution.py:20
  8.2 10.2 %collective-permute-start.1 = (f32[6,16,1]{2,1,0:T(8,128)S(1)}, f32[6,16,1]{2,1,0:T(8,128)S(1)}, u32[]{:S(2)}, u32[]{:S(2)}) collective-permute-start(f32[6,16,1]{2,1,0:T(8,128)S(1)} %get-tuple-element.31), channel_id=1, source_target_pairs={{1,0},{2,1},{3,2},{4,3},{5,4},{6,5},{7,6},{8,7},{9,8},{10,9},{11,1... | collective-permute-start | bytes 1160 | tf_op jit(solution)/shard_map/ppermute | solution.py:21
  18.6 8.1 %collective-permute-start.3 = (f32[6,1,130]{2,1,0:T(1,128)S(1)}, f32[6,1,130]{2,1,0:T(1,128)S(1)}, u32[]{:S(2)}, u32[]{:S(2)}) collective-permute-start(f32[6,1,130]{2,1,0:T(1,128)S(1)} %get-tuple-element.26), channel_id=1, source_target_pairs={{16,0},{32,16},{48,32},{64,48},{80,64},{96,80},{112,96},{17,1},{33... | collective-permute-start | bytes 9368 | tf_op jit(solution)/shard_map/ppermute | solution.py:21
  24.0 7.6 %collective-permute-start.2 = (f32[6,1,130]{2,1,0:T(1,128)S(1)}, f32[6,1,130]{2,1,0:T(1,128)S(1)}, u32[]{:S(2)}, u32[]{:S(2)}) collective-permute-start(f32[6,1,130]{2,1,0:T(1,128)S(1)} %get-tuple-element.27), channel_id=1, source_target_pairs={{0,16},{16,32},{32,48},{48,64},{64,80},{80,96},{96,112},{1,17},{17... | collective-permute-start | bytes 9368 | tf_op jit(solution)/shard_map/ppermute | solution.py:20
  26.7 25.1 %copy-start.14 = (f32[16,128]{1,0:T(8,128)}, f32[16,128]{1,0:T(8,128)S(1)}, u32[]{:S(2)}) copy-start(f32[16,128]{1,0:T(8,128)S(1)} %convert_element_type.70) | copy-start | bytes 24580
  35.5 4.7 %collective-permute-start.4 = (f32[6,16,1]{2,1,0:T(8,128)S(1)}, f32[6,16,1]{2,1,0:T(8,128)S(1)}, u32[]{:S(2)}, u32[]{:S(2)}) collective-permute-start(f32[6,16,1]{2,1,0:T(8,128)S(1)} %get-tuple-element.28), channel_id=1, source_target_pairs={{0,1},{1,2},{2,3},{3,4},{4,5},{5,6},{6,7},{7,8},{8,9},{9,10},{10,1... | collective-permute-start | bytes 1160 | tf_op jit(solution)/shard_map/ppermute | solution.py:20
  35.5 4.7 %collective-permute-start.5 = (f32[6,16,1]{2,1,0:T(8,128)S(1)}, f32[6,16,1]{2,1,0:T(8,128)S(1)}, u32[]{:S(2)}, u32[]{:S(2)}) collective-permute-start(f32[6,16,1]{2,1,0:T(8,128)S(1)} %get-tuple-element.29), channel_id=1, source_target_pairs={{1,0},{2,1},{3,2},{4,3},{5,4},{6,5},{7,6},{8,7},{9,8},{10,9},{11,1... | collective-permute-start | bytes 1160 | tf_op jit(solution)/shard_map/ppermute | solution.py:21
  40.4 6.1 %collective-permute-start.7 = (f32[6,1,130]{2,1,0:T(1,128)S(1)}, f32[6,1,130]{2,1,0:T(1,128)S(1)}, u32[]{:S(2)}, u32[]{:S(2)}) collective-permute-start(f32[6,1,130]{2,1,0:T(1,128)S(1)} %get-tuple-element.22), channel_id=1, source_target_pairs={{16,0},{32,16},{48,32},{64,48},{80,64},{96,80},{112,96},{17,1},{33... | collective-permute-start | bytes 9368 | tf_op jit(solution)/shard_map/ppermute | solution.py:21
  42.3 7.6 %collective-permute-start.6 = (f32[6,1,130]{2,1,0:T(1,128)S(1)}, f32[6,1,130]{2,1,0:T(1,128)S(1)}, u32[]{:S(2)}, u32[]{:S(2)}) collective-permute-start(f32[6,1,130]{2,1,0:T(1,128)S(1)} %get-tuple-element.23), channel_id=1, source_target_pairs={{0,16},{16,32},{32,48},{48,64},{64,80},{80,96},{96,112},{1,17},{17... | collective-permute-start | bytes 9368 | tf_op jit(solution)/shard_map/ppermute | solution.py:20
  70.0 8.9 %collective-permute-start.8 = (f32[54,16,1]{2,1,0:T(8,128)S(1)}, f32[54,16,1]{2,1,0:T(8,128)S(1)}, u32[]{:S(2)}, u32[]{:S(2)}) collective-permute-start(f32[54,16,1]{2,1,0:T(8,128)S(1)} %get-tuple-element.18), channel_id=1, source_target_pairs={{0,1},{1,2},{2,3},{3,4},{4,5},{5,6},{6,7},{7,8},{8,9},{9,10},{10,1... | collective-permute-start | bytes 10376 | tf_op jit(solution)/shard_map/ppermute | solution.py:20
  70.0 8.9 %collective-permute-start.9 = (f32[54,16,1]{2,1,0:T(8,128)S(1)}, f32[54,16,1]{2,1,0:T(8,128)S(1)}, u32[]{:S(2)}, u32[]{:S(2)}) collective-permute-start(f32[54,16,1]{2,1,0:T(8,128)S(1)} %get-tuple-element.19), channel_id=1, source_target_pairs={{1,0},{2,1},{3,2},{4,3},{5,4},{6,5},{7,6},{8,7},{9,8},{10,9},{11,1... | collective-permute-start | bytes 10376 | tf_op jit(solution)/shard_map/ppermute | solution.py:21
  74.0 12.2 %copy-start.5 = (f32[1,6,16,128]{3,2,1,0:T(8,128)S(1)}, f32[1,6,16,128]{3,2,1,0:T(8,128)}, u32[]{:S(2)}) copy-start(f32[1,6,16,128]{3,2,1,0:T(8,128)} %copy-done.4) | copy-start | bytes 147460
  80.0 6.5 %collective-permute-start.10 = (f32[54,1,130]{2,1,0:T(1,128)}, f32[54,1,130]{2,1,0:T(1,128)S(1)}, u32[]{:S(2)}, u32[]{:S(2)}) collective-permute-start(f32[54,1,130]{2,1,0:T(1,128)} %get-tuple-element.14), channel_id=1, source_target_pairs={{16,0},{32,16},{48,32},{64,48},{80,64},{96,80},{112,96},{17,1},{33... | collective-permute-start | bytes 84248 | tf_op jit(solution)/shard_map/ppermute | solution.py:21
  82.1 8.6 %collective-permute-start.11 = (f32[54,1,130]{2,1,0:T(1,128)}, f32[54,1,130]{2,1,0:T(1,128)}, u32[]{:S(2)}, u32[]{:S(2)}) collective-permute-start(f32[54,1,130]{2,1,0:T(1,128)} %get-tuple-element.15), channel_id=1, source_target_pairs={{0,16},{16,32},{32,48},{48,64},{64,80},{80,96},{96,112},{1,17},{17... | collective-permute-start | bytes 84248 | tf_op jit(solution)/shard_map/ppermute | solution.py:20
  95.1 8.9 %collective-permute-start.12 = (f32[54,16,1]{2,1,0:T(8,128)S(1)}, f32[54,16,1]{2,1,0:T(8,128)S(1)}, u32[]{:S(2)}, u32[]{:S(2)}) collective-permute-start(f32[54,16,1]{2,1,0:T(8,128)S(1)} %get-tuple-element.16), channel_id=1, source_target_pairs={{0,1},{1,2},{2,3},{3,4},{4,5},{5,6},{6,7},{7,8},{8,9},{9,10},{10,1... | collective-permute-start | bytes 10376 | tf_op jit(solution)/shard_map/ppermute | solution.py:20
  95.1 8.9 %collective-permute-start.13 = (f32[54,16,1]{2,1,0:T(8,128)S(1)}, f32[54,16,1]{2,1,0:T(8,128)S(1)}, u32[]{:S(2)}, u32[]{:S(2)}) collective-permute-start(f32[54,16,1]{2,1,0:T(8,128)S(1)} %get-tuple-element.17), channel_id=1, source_target_pairs={{1,0},{2,1},{3,2},{4,3},{5,4},{6,5},{7,6},{8,7},{9,8},{10,9},{11,1... | collective-permute-start | bytes 10376 | tf_op jit(solution)/shard_map/ppermute | solution.py:21
  104.5 101.4 %collective-permute-start.14 = (f32[54,1,130]{2,1,0:T(1,128)S(1)}, f32[54,1,130]{2,1,0:T(1,128)S(1)}, u32[]{:S(2)}, u32[]{:S(2)}) collective-permute-start(f32[54,1,130]{2,1,0:T(1,128)S(1)} %get-tuple-element.12), channel_id=1, source_target_pairs={{16,0},{32,16},{48,32},{64,48},{80,64},{96,80},{112,96},{17,1},{33... | collective-permute-start | bytes 84248 | tf_op jit(solution)/shard_map/ppermute | solution.py:21
  106.4 99.5 %collective-permute-start.15 = (f32[54,1,130]{2,1,0:T(1,128)S(1)}, f32[54,1,130]{2,1,0:T(1,128)S(1)}, u32[]{:S(2)}, u32[]{:S(2)}) collective-permute-start(f32[54,1,130]{2,1,0:T(1,128)S(1)} %get-tuple-element.13), channel_id=1, source_target_pairs={{0,16},{16,32},{32,48},{48,64},{64,80},{80,96},{96,112},{1,17},{17... | collective-permute-start | bytes 84248 | tf_op jit(solution)/shard_map/ppermute | solution.py:20
  205.1 86.4 %all-reduce.5.cloned.1.call-start = ((), (), s32[]{:S(2)}) async-start(), calls=%async_computation.1 | async-start | bytes 196608 | tf_op jit(solution)/shard_map/psum | solution.py:170
  205.9 89.2 %copy-start.16 = (f32[24064]{0:T(1024)S(1)}, f32[24064]{0:T(1024)}, u32[]{:S(2)}) copy-start(f32[24064]{0:T(1024)} %param.17) | copy-start | bytes 288772
  226.9 68.2 %copy-start.8 = (bf16[128,128]{1,0:T(8,128)(2,1)S(1)}, bf16[128,128]{1,0:T(8,128)(2,1)}, u32[]{:S(2)}) copy-start(bf16[128,128]{1,0:T(8,128)(2,1)} %param.14) | copy-start | bytes 98308
  (15 other events, 34.2 us)
Sparse Core Ops, SparseCore 0:
  98.9 104.6 all-reduce.2
  209.1 82.3 all-reduce.4
where the time goes:
time: 306 us; the launch traced here: 305 us
  waiting for transfers between devices  184 us (60%)
  starting transfers between devices  42.6 us (14%)
  local copies, waits for them, and re-layouts  20.1 us (7%)
  blocking collectives  20.1 us (7%)
  between operations  17.7 us (6%)
  other arithmetic  10.5 us (3%)
  matrix products  9.52 us (3%)
    psum x1, waiting for transfers between devices, on_device(): band = lax.psum(local_grad, 'lon')  93.3 us
    psum x1, waiting for transfers between devices, on_device(): total_grad, band_square = lax.psum((band, jnp.sum(band * band)), 'lat')  64.6 us
    ppermute x8, starting transfers between devices, with_halo(): after = lax.ppermute(first, axis, down)  28.7 us
    ppermute x8, waiting for transfers between devices, with_halo(): before = lax.ppermute(last, axis, up)  25.5 us
    psum x1, blocking collectives, on_device(): total_grad, band_square = lax.psum((band, jnp.sum(band * band)), 'lat')  20.1 us
    ppermute x8, starting transfers between devices, with_halo(): before = lax.ppermute(last, axis, up)  13.9 us
    concatenate x2, local copies, waits for them, and re-layouts, backward_block(): jnp.concatenate([blank, spread, blank, spread, direct - 4.0 * spread, spr...  12.4 us
  transfers between devices with their start and end apart: 18, of which 9 were waited for; matrix products, arithmetic and copies ran while one was open for 2% of the time, Pallas kernels for 0%

commit v1 on v0

--- a/solution.py
+++ b/solution.py
@@ -166,7 +166,7 @@
             )
         adjoint = total
     params_count = local_grad.shape[0]
-    band = lax.psum(local_grad, "lon")
+    band = jnp.sum(lax.all_gather(local_grad, "lon"), 0)
     total_grad, band_square = lax.psum((band, jnp.sum(band * band)), "lat")
     grad_square = jnp.sum(total_grad * total_grad)
     noise_ratio = (band_square / (grad_square + epsilon)).reshape(1)

time: 306 us -> 222 us (0.73)
  waiting for transfers between devices: 184 us -> 112 us
  local copies, waits for them, and re-layouts: 20.1 us -> 4.39 us
  other arithmetic: 10.5 us -> 16.8 us
    psum x1 -> x0, waiting for transfers between devices: 93.3 us -> none  [on_device(): band = lax.psum(local_grad, 'lon')]
    all_gather x0 -> x1, waiting for transfers between devices: none -> 20 us  [on_device(): band = jnp.sum(lax.all_gather(local_grad, 'lon'), 0)]
    concatenate x2, local copies, waits for them, and re-layouts: 12.4 us -> 1.13 us  [backward_block(): jnp.concatenate([blank, spread, blank, spread, direct - 4.0 * spread, spr...]
    unnamed x61 -> x37, local copies, waits for them, and re-layouts: 4.9 us -> 1.1 us
    unnamed x8 -> x9, other arithmetic: 2.13 us -> 5.38 us
  transfers between devices with their start and end apart: 18 -> 18, of which waited for: 9 -> 11; matrix products, arithmetic and copies ran while one was open for 2% -> 4% of each run, Pallas kernels for 0% -> 0%
where the time goes in v1:
time: 222 us; the launch traced here: 221 us
  waiting for transfers between devices  112 us (50%)
  starting transfers between devices  42.4 us (19%)
  blocking collectives  20.2 us (9%)
  between operations  17.7 us (8%)
  other arithmetic  16.8 us (8%)
  matrix products  7.42 us (3%)
  local copies, waits for them, and re-layouts  4.39 us (2%)
    psum x1, waiting for transfers between devices, on_device(): total_grad, band_square = lax.psum((band, jnp.sum(band * band)), 'lat')  63 us
    ppermute x8, starting transfers between devices, with_halo(): after = lax.ppermute(first, axis, down)  28.7 us
    ppermute x8, waiting for transfers between devices, with_halo(): before = lax.ppermute(last, axis, up)  27.1 us
    psum x1, blocking collectives, on_device(): total_grad, band_square = lax.psum((band, jnp.sum(band * band)), 'lat')  20.2 us
    all_gather x1, waiting for transfers between devices, on_device(): band = jnp.sum(lax.all_gather(local_grad, 'lon'), 0)  20 us
    ppermute x8, starting transfers between devices, with_halo(): before = lax.ppermute(last, axis, up)  13.7 us
    unnamed x9, other arithmetic  5.38 us
  transfers between devices with their start and end apart: 18, of which 11 were waited for; matrix products, arithmetic and copies ran while one was open for 4% of the time, Pallas kernels for 0%

profile of v1, /device:TPU:40, one launch (start us, length us, event | category | flops | bytes accessed | tf_op | source)
XLA Modules:
  0.0 220.8 jit_solution(1539568956006518721)
XLA Ops:
  8.2 8.5 %collective-permute-start.1 = (f32[6,16,1]{2,1,0:T(8,128)S(1)}, f32[6,16,1]{2,1,0:T(8,128)S(1)}, u32[]{:S(2)}, u32[]{:S(2)}) collective-permute-start(f32[6,16,1]{2,1,0:T(8,128)S(1)} %get-tuple-element.31), channel_id=1, source_target_pairs={{1,0},{2,1},{3,2},{4,3},{5,4},{6,5},{7,6},{8,7},{9,8},{10,9},{11,1... | collective-permute-start | bytes 1160 | tf_op jit(solution)/shard_map/ppermute | solution.py:21
  16.7 1.8 collective-permute-done
  19.3 5.5 %collective-permute-start.3 = (f32[6,1,130]{2,1,0:T(1,128)S(1)}, f32[6,1,130]{2,1,0:T(1,128)S(1)}, u32[]{:S(2)}, u32[]{:S(2)}) collective-permute-start(f32[6,1,130]{2,1,0:T(1,128)S(1)} %get-tuple-element.26), channel_id=1, source_target_pairs={{16,0},{32,16},{48,32},{64,48},{80,64},{96,80},{112,96},{17,1},{33... | collective-permute-start | bytes 9368 | tf_op jit(solution)/shard_map/ppermute | solution.py:21
  24.8 1.9 collective-permute-start.2
  28.4 4.0 %collective-permute-done.2 = f32[6,1,130]{2,1,0:T(1,128)S(1)} collective-permute-done((f32[6,1,130]{2,1,0:T(1,128)S(1)}, f32[6,1,130]{2,1,0:T(1,128)S(1)}, u32[]{:S(2)}, u32[]{:S(2)}) %collective-permute-start.2) | collective-permute-done | bytes 3152 | tf_op jit(solution)/shard_map/ppermute | solution.py:20
  37.8 3.0 %collective-permute-start.5 = (f32[6,16,1]{2,1,0:T(8,128)S(1)}, f32[6,16,1]{2,1,0:T(8,128)S(1)}, u32[]{:S(2)}, u32[]{:S(2)}) collective-permute-start(f32[6,16,1]{2,1,0:T(8,128)S(1)} %get-tuple-element.29), channel_id=1, source_target_pairs={{1,0},{2,1},{3,2},{4,3},{5,4},{6,5},{7,6},{8,7},{9,8},{10,9},{11,1... | collective-permute-start | bytes 1160 | tf_op jit(solution)/shard_map/ppermute | solution.py:21
  40.7 1.8 collective-permute-done.4
  42.6 2.0 collective-permute-start.7
  44.7 3.8 %collective-permute-start.6 = (f32[6,1,130]{2,1,0:T(1,128)S(1)}, f32[6,1,130]{2,1,0:T(1,128)S(1)}, u32[]{:S(2)}, u32[]{:S(2)}) collective-permute-start(f32[6,1,130]{2,1,0:T(1,128)S(1)} %get-tuple-element.23), channel_id=1, source_target_pairs={{0,16},{16,32},{32,48},{48,64},{64,80},{80,96},{96,112},{1,17},{17... | collective-permute-start | bytes 9368 | tf_op jit(solution)/shard_map/ppermute | solution.py:20
  48.7 3.6 %collective-permute-done.6 = f32[6,1,130]{2,1,0:T(1,128)S(1)} collective-permute-done((f32[6,1,130]{2,1,0:T(1,128)S(1)}, f32[6,1,130]{2,1,0:T(1,128)S(1)}, u32[]{:S(2)}, u32[]{:S(2)}) %collective-permute-start.6) | collective-permute-done | bytes 3152 | tf_op jit(solution)/shard_map/ppermute | solution.py:20
  57.9 2.9 %collective-permute-start.9 = (f32[54,16,1]{2,1,0:T(8,128)S(1)}, f32[54,16,1]{2,1,0:T(8,128)S(1)}, u32[]{:S(2)}, u32[]{:S(2)}) collective-permute-start(f32[54,16,1]{2,1,0:T(8,128)S(1)} %get-tuple-element.19), channel_id=1, source_target_pairs={{1,0},{2,1},{3,2},{4,3},{5,4},{6,5},{7,6},{8,7},{9,8},{10,9},{11,1... | collective-permute-start | bytes 10376 | tf_op jit(solution)/shard_map/ppermute | solution.py:21
  60.9 5.9 %collective-permute-done.8 = f32[54,16,1]{2,1,0:T(8,128)S(1)} collective-permute-done((f32[54,16,1]{2,1,0:T(8,128)S(1)}, f32[54,16,1]{2,1,0:T(8,128)S(1)}, u32[]{:S(2)}, u32[]{:S(2)}) %collective-permute-start.8) | collective-permute-done | bytes 3488 | tf_op jit(solution)/shard_map/ppermute | solution.py:20
  67.9 1.9 collective-permute-start.10
  69.8 3.9 %collective-permute-start.11 = (f32[54,1,130]{2,1,0:T(1,128)}, f32[54,1,130]{2,1,0:T(1,128)}, u32[]{:S(2)}, u32[]{:S(2)}) collective-permute-start(f32[54,1,130]{2,1,0:T(1,128)} %get-tuple-element.15), channel_id=1, source_target_pairs={{0,16},{16,32},{32,48},{48,64},{64,80},{80,96},{96,112},{1,17},{17... | collective-permute-start | bytes 84248 | tf_op jit(solution)/shard_map/ppermute | solution.py:20
  74.2 4.0 %collective-permute-done.11 = f32[54,1,130]{2,1,0:T(1,128)} collective-permute-done((f32[54,1,130]{2,1,0:T(1,128)}, f32[54,1,130]{2,1,0:T(1,128)}, u32[]{:S(2)}, u32[]{:S(2)}) %collective-permute-start.11) | collective-permute-done | bytes 28112 | tf_op jit(solution)/shard_map/ppermute | solution.py:20
  83.7 2.9 %collective-permute-start.13 = (f32[54,16,1]{2,1,0:T(8,128)S(1)}, f32[54,16,1]{2,1,0:T(8,128)S(1)}, u32[]{:S(2)}, u32[]{:S(2)}) collective-permute-start(f32[54,16,1]{2,1,0:T(8,128)S(1)} %get-tuple-element.17), channel_id=1, source_target_pairs={{1,0},{2,1},{3,2},{4,3},{5,4},{6,5},{7,6},{8,7},{9,8},{10,9},{11,1... | collective-permute-start | bytes 10376 | tf_op jit(solution)/shard_map/ppermute | solution.py:21
  86.7 5.9 %collective-permute-done.12 = f32[54,16,1]{2,1,0:T(8,128)S(1)} collective-permute-done((f32[54,16,1]{2,1,0:T(8,128)S(1)}, f32[54,16,1]{2,1,0:T(8,128)S(1)}, u32[]{:S(2)}, u32[]{:S(2)}) %collective-permute-start.12) | collective-permute-done | bytes 3488 | tf_op jit(solution)/shard_map/ppermute | solution.py:20
  93.9 1.9 collective-permute-start.14
  95.9 4.1 %collective-permute-start.15 = (f32[54,1,130]{2,1,0:T(1,128)S(1)}, f32[54,1,130]{2,1,0:T(1,128)S(1)}, u32[]{:S(2)}, u32[]{:S(2)}) collective-permute-start(f32[54,1,130]{2,1,0:T(1,128)S(1)} %get-tuple-element.13), channel_id=1, source_target_pairs={{0,16},{16,32},{32,48},{48,64},{64,80},{80,96},{96,112},{1,17},{17... | collective-permute-start | bytes 84248 | tf_op jit(solution)/shard_map/ppermute | solution.py:20
  100.0 20.0 %all-gather.3.cloned.1.call-done = f32[16,1,24064]{2,1,0:T(1,128)} async-done(((f32[1,1,24064]{2,1,0:T(1,128)}), f32[16,1,24064]{2,1,0:T(1,128)}) %all-gather.3.cloned.1.call-update) | async-done | bytes 1540112 | tf_op jit(solution)/shard_map/all_gather | solution.py:169
  119.9 2.4 %reduce_sum.27 = f32[24064]{0:T(1024)S(1)} reduce(f32[16,1,24064]{2,1,0:T(1,128)} %all-gather.3.cloned.1.call-done, f32[]{:T(128)} %constant.1.clone.1), dimensions={0,1}, to_apply=%region_0.0 | reduce | flops 360960 | bytes 1636356 | tf_op jit(solution)/shard_map/reduce_sum | solution.py:169
  124.6 20.2 %psum.15 = f32[]{:T(128)} all-reduce(f32[]{:T(128)} %multiply_reduce_fusion), channel_id=1, replica_groups=mesh['ens'=4,'lat'=8,'lon'=16] {'lat'}, use_global_device_ids=true, to_apply=%region_4.0 | all-reduce | flops 1 | bytes 8 | tf_op jit(solution)/shard_map/psum | solution.py:170
  144.8 63.0 %all-reduce.2.cloned.1.call-done = f32[24064]{0:T(1024)} async-done(((f32[24064]{0:T(1024)}), f32[24064]{0:T(1024)}) %all-reduce.2.cloned.1.call-update) | async-done | bytes 96272 | tf_op jit(solution)/shard_map/psum | solution.py:170
  211.3 1.6 subtract_add_fusion
  (113 shorter events, 26.6 us)
Async XLA Ops:
  7.2 19.5 %copy-start = (f32[6,6]{1,0:T(8,128)S(1)}, f32[6,6]{1,0:T(8,128)}, u32[]{:S(2)}) copy-start(f32[6,6]{1,0:T(8,128)} %param.11) | copy-start | bytes 436
  7.2 29.4 %copy-start.4 = (bf16[128,54]{0,1:T(8,128)(2,1)S(1)}, bf16[128,54]{0,1:T(8,128)(2,1)}, u32[]{:S(2)}) copy-start(bf16[128,54]{0,1:T(8,128)(2,1)} %param.13) | copy-start | bytes 41476
  7.2 112.7 %all-gather.3.cloned.1.call-start = ((), (), s32[]{:S(2)}) async-start(), calls=%async_computation.1 | async-start | bytes 1636352 | tf_op jit(solution)/shard_map/all_gather | solution.py:169
  8.2 10.3 %collective-permute-start = (f32[6,16,1]{2,1,0:T(8,128)S(1)}, f32[6,16,1]{2,1,0:T(8,128)S(1)}, u32[]{:S(2)}, u32[]{:S(2)}) collective-permute-start(f32[6,16,1]{2,1,0:T(8,128)S(1)} %get-tuple-element.30), channel_id=1, source_target_pairs={{0,1},{1,2},{2,3},{3,4},{4,5},{5,6},{6,7},{7,8},{8,9},{9,10},{10,1... | collective-permute-start | bytes 1160 | tf_op jit(solution)/shard_map/ppermute | solution.py:20
  8.2 10.2 %collective-permute-start.1 = (f32[6,16,1]{2,1,0:T(8,128)S(1)}, f32[6,16,1]{2,1,0:T(8,128)S(1)}, u32[]{:S(2)}, u32[]{:S(2)}) collective-permute-start(f32[6,16,1]{2,1,0:T(8,128)S(1)} %get-tuple-element.31), channel_id=1, source_target_pairs={{1,0},{2,1},{3,2},{4,3},{5,4},{6,5},{7,6},{8,7},{9,8},{10,9},{11,1... | collective-permute-start | bytes 1160 | tf_op jit(solution)/shard_map/ppermute | solution.py:21
  19.3 17.7 %copy-start.3 = (bf16[128,128]{1,0:T(8,128)(2,1)S(1)}, bf16[128,128]{1,0:T(8,128)(2,1)}, u32[]{:S(2)}) copy-start(bf16[128,128]{1,0:T(8,128)(2,1)} %param.14) | copy-start | bytes 98308
  19.3 9.1 %collective-permute-start.3 = (f32[6,1,130]{2,1,0:T(1,128)S(1)}, f32[6,1,130]{2,1,0:T(1,128)S(1)}, u32[]{:S(2)}, u32[]{:S(2)}) collective-permute-start(f32[6,1,130]{2,1,0:T(1,128)S(1)} %get-tuple-element.26), channel_id=1, source_target_pairs={{16,0},{32,16},{48,32},{64,48},{80,64},{96,80},{112,96},{17,1},{33... | collective-permute-start | bytes 9368 | tf_op jit(solution)/shard_map/ppermute | solution.py:21
  24.8 7.6 %collective-permute-start.2 = (f32[6,1,130]{2,1,0:T(1,128)S(1)}, f32[6,1,130]{2,1,0:T(1,128)S(1)}, u32[]{:S(2)}, u32[]{:S(2)}) collective-permute-start(f32[6,1,130]{2,1,0:T(1,128)S(1)} %get-tuple-element.27), channel_id=1, source_target_pairs={{0,16},{16,32},{32,48},{48,64},{64,80},{80,96},{96,112},{1,17},{17... | collective-permute-start | bytes 9368 | tf_op jit(solution)/shard_map/ppermute | solution.py:20
  34.5 2.7 %copy-start.8 = (bf16[6,128]{1,0:T(8,128)(2,1)S(1)}, bf16[6,128]{1,0:T(8,128)(2,1)}, u32[]{:S(2)}) copy-start(bf16[6,128]{1,0:T(8,128)(2,1)} %param.15) | copy-start | bytes 4612
  36.5 1.0 copy-start.1
  37.8 4.7 %collective-permute-start.4 = (f32[6,16,1]{2,1,0:T(8,128)S(1)}, f32[6,16,1]{2,1,0:T(8,128)S(1)}, u32[]{:S(2)}, u32[]{:S(2)}) collective-permute-start(f32[6,16,1]{2,1,0:T(8,128)S(1)} %get-tuple-element.28), channel_id=1, source_target_pairs={{0,1},{1,2},{2,3},{3,4},{4,5},{5,6},{6,7},{7,8},{8,9},{9,10},{10,1... | collective-permute-start | bytes 1160 | tf_op jit(solution)/shard_map/ppermute | solution.py:20
  37.8 4.7 %collective-permute-start.5 = (f32[6,16,1]{2,1,0:T(8,128)S(1)}, f32[6,16,1]{2,1,0:T(8,128)S(1)}, u32[]{:S(2)}, u32[]{:S(2)}) collective-permute-start(f32[6,16,1]{2,1,0:T(8,128)S(1)} %get-tuple-element.29), channel_id=1, source_target_pairs={{1,0},{2,1},{3,2},{4,3},{5,4},{6,5},{7,6},{8,7},{9,8},{10,9},{11,1... | collective-permute-start | bytes 1160 | tf_op jit(solution)/shard_map/ppermute | solution.py:21
  42.6 6.1 %collective-permute-start.7 = (f32[6,1,130]{2,1,0:T(1,128)S(1)}, f32[6,1,130]{2,1,0:T(1,128)S(1)}, u32[]{:S(2)}, u32[]{:S(2)}) collective-permute-start(f32[6,1,130]{2,1,0:T(1,128)S(1)} %get-tuple-element.22), channel_id=1, source_target_pairs={{16,0},{32,16},{48,32},{64,48},{80,64},{96,80},{112,96},{17,1},{33... | collective-permute-start | bytes 9368 | tf_op jit(solution)/shard_map/ppermute | solution.py:21
  44.7 7.6 %collective-permute-start.6 = (f32[6,1,130]{2,1,0:T(1,128)S(1)}, f32[6,1,130]{2,1,0:T(1,128)S(1)}, u32[]{:S(2)}, u32[]{:S(2)}) collective-permute-start(f32[6,1,130]{2,1,0:T(1,128)S(1)} %get-tuple-element.23), channel_id=1, source_target_pairs={{0,16},{16,32},{32,48},{48,64},{64,80},{80,96},{96,112},{1,17},{17... | collective-permute-start | bytes 9368 | tf_op jit(solution)/shard_map/ppermute | solution.py:20
  57.9 8.9 %collective-permute-start.8 = (f32[54,16,1]{2,1,0:T(8,128)S(1)}, f32[54,16,1]{2,1,0:T(8,128)S(1)}, u32[]{:S(2)}, u32[]{:S(2)}) collective-permute-start(f32[54,16,1]{2,1,0:T(8,128)S(1)} %get-tuple-element.18), channel_id=1, source_target_pairs={{0,1},{1,2},{2,3},{3,4},{4,5},{5,6},{6,7},{7,8},{8,9},{9,10},{10,1... | collective-permute-start | bytes 10376 | tf_op jit(solution)/shard_map/ppermute | solution.py:20
  57.9 8.9 %collective-permute-start.9 = (f32[54,16,1]{2,1,0:T(8,128)S(1)}, f32[54,16,1]{2,1,0:T(8,128)S(1)}, u32[]{:S(2)}, u32[]{:S(2)}) collective-permute-start(f32[54,16,1]{2,1,0:T(8,128)S(1)} %get-tuple-element.19), channel_id=1, source_target_pairs={{1,0},{2,1},{3,2},{4,3},{5,4},{6,5},{7,6},{8,7},{9,8},{10,9},{11,1... | collective-permute-start | bytes 10376 | tf_op jit(solution)/shard_map/ppermute | solution.py:21
  67.9 6.4 %collective-permute-start.10 = (f32[54,1,130]{2,1,0:T(1,128)}, f32[54,1,130]{2,1,0:T(1,128)}, u32[]{:S(2)}, u32[]{:S(2)}) collective-permute-start(f32[54,1,130]{2,1,0:T(1,128)} %get-tuple-element.14), channel_id=1, source_target_pairs={{16,0},{32,16},{48,32},{64,48},{80,64},{96,80},{112,96},{17,1},{33... | collective-permute-start | bytes 84248 | tf_op jit(solution)/shard_map/ppermute | solution.py:21
  69.8 8.5 %collective-permute-start.11 = (f32[54,1,130]{2,1,0:T(1,128)}, f32[54,1,130]{2,1,0:T(1,128)}, u32[]{:S(2)}, u32[]{:S(2)}) collective-permute-start(f32[54,1,130]{2,1,0:T(1,128)} %get-tuple-element.15), channel_id=1, source_target_pairs={{0,16},{16,32},{32,48},{48,64},{64,80},{80,96},{96,112},{1,17},{17... | collective-permute-start | bytes 84248 | tf_op jit(solution)/shard_map/ppermute | solution.py:20
  83.7 8.9 %collective-permute-start.12 = (f32[54,16,1]{2,1,0:T(8,128)S(1)}, f32[54,16,1]{2,1,0:T(8,128)S(1)}, u32[]{:S(2)}, u32[]{:S(2)}) collective-permute-start(f32[54,16,1]{2,1,0:T(8,128)S(1)} %get-tuple-element.16), channel_id=1, source_target_pairs={{0,1},{1,2},{2,3},{3,4},{4,5},{5,6},{6,7},{7,8},{8,9},{9,10},{10,1... | collective-permute-start | bytes 10376 | tf_op jit(solution)/shard_map/ppermute | solution.py:20
  83.7 9.8 %collective-permute-start.13 = (f32[54,16,1]{2,1,0:T(8,128)S(1)}, f32[54,16,1]{2,1,0:T(8,128)S(1)}, u32[]{:S(2)}, u32[]{:S(2)}) collective-permute-start(f32[54,16,1]{2,1,0:T(8,128)S(1)} %get-tuple-element.17), channel_id=1, source_target_pairs={{1,0},{2,1},{3,2},{4,3},{5,4},{6,5},{7,6},{8,7},{9,8},{10,9},{11,1... | collective-permute-start | bytes 10376 | tf_op jit(solution)/shard_map/ppermute | solution.py:21
  93.9 29.7 %collective-permute-start.14 = (f32[54,1,130]{2,1,0:T(1,128)S(1)}, f32[54,1,130]{2,1,0:T(1,128)S(1)}, u32[]{:S(2)}, u32[]{:S(2)}) collective-permute-start(f32[54,1,130]{2,1,0:T(1,128)S(1)} %get-tuple-element.12), channel_id=1, source_target_pairs={{16,0},{32,16},{48,32},{64,48},{80,64},{96,80},{112,96},{17,1},{33... | collective-permute-start | bytes 84248 | tf_op jit(solution)/shard_map/ppermute | solution.py:21
  95.9 115.4 %copy-start.6 = (f32[24064]{0:T(1024)S(1)}, f32[24064]{0:T(1024)}, u32[]{:S(2)}) copy-start(f32[24064]{0:T(1024)} %param.17) | copy-start | bytes 288772
  95.9 27.8 %collective-permute-start.15 = (f32[54,1,130]{2,1,0:T(1,128)S(1)}, f32[54,1,130]{2,1,0:T(1,128)S(1)}, u32[]{:S(2)}, u32[]{:S(2)}) collective-permute-start(f32[54,1,130]{2,1,0:T(1,128)S(1)} %get-tuple-element.13), channel_id=1, source_target_pairs={{0,16},{16,32},{32,48},{48,64},{64,80},{80,96},{96,112},{1,17},{17... | collective-permute-start | bytes 84248 | tf_op jit(solution)/shard_map/ppermute | solution.py:20
  122.9 84.9 %all-reduce.2.cloned.1.call-start = ((), (), s32[]{:S(2)}) async-start(), calls=%async_computation | async-start | bytes 196608 | tf_op jit(solution)/shard_map/psum | solution.py:170
  (3 other events, 2.7 us)
Sparse Core Ops, SparseCore 0:
  82.0 37.9 all-gather.2
  127.3 80.5 all-reduce.1
